TPU v7x, 32 devices: a whole 2x2x4 slice. The times are simulated.
32 devices in a mesh: groups: 2 (over x), store: 16 (over z, y, core).
Axes of the slice: x: 2, y: 2, z: 4, core: 2. Of those that a mesh axis runs over, the one named last changes fastest.
Arguments:
- sources: bfloat16 [16384, 512], P(('groups', 'store')), parts along dimension 0, may hold values from -1800 to 1800
- self_terms: float32 [2, 8192], P(None, 'store'), may hold values from 0.5 to 2
- near_tiles: bfloat16 [2, 32, 5, 256, 256], P(None, 'store'), may hold values from -1 to 1
- near_cols: int32 [32, 5], P('store'), may hold values from 0 to 31, as said below
- near_count: int32 [32], P('store'), may hold values from 1 to 5, as said below
- far_cols: int32 [32, 6], P('store'), may hold values from 0 to 31, as said below
- basis_left: bfloat16 [32, 256, 32], P('store'), may hold values from -2 to 2
- basis_right: bfloat16 [32, 256, 32], P('store'), may hold values from -2 to 2
- couplings: bfloat16 [2, 32, 6, 32, 32], P(None, 'store'), may hold values from -1 to 1
Outputs:
- images: float32 [2, 16384, 512], P(None, ('groups', 'store')), parts along dimension 1
- heights: float32 [4, 512], P('groups'), parts along dimension 0
- norms: float32 [4, 512], P('groups'), parts along dimension 0
There are 2 independent parts, one for each index of `groups`. A program takes and returns all parts, laid end to end along the dimension named above; an argument that names none is the same for every part. Nothing has to cross between parts.
Inputs may be any that keep to these rules, and one draw needn't show every extreme that they name: `near_cols`: the slots of row block i name the blocks i - 2 to i + 2, cyclically, each once, in a drawn order. Slots 0 to near_count - 1 of a row block are live; block 0 has all 5. `far_cols`: a far-field block lies more than 2 blocks from its row block, cyclically.
All inputs are finite; a program needn't handle non-finite values.
Results may differ from a plain program's by a relative error of at most 0.011.
Values may be sent and summed in bfloat16 or wider, within the bound.
A program may use at most 128 MiB of HBM per device.

v0:
```python
import jax
import jax.numpy as jnp
from jax import lax
from jax.sharding import PartitionSpec as P

REACH = 2


EPSILON = 1e-06


def padded_2(block, sides, width):
    for axis, dim in sides:
        count = lax.axis_size(axis)
        forward = [(i, i + 1) for i in range(count - 1)]
        forward.append((count - 1, 0))
        backward = [(target, source) for source, target in forward]
        low = lax.ppermute(
            lax.slice_in_dim(block, block.shape[dim] - width, None, axis=dim), axis, forward
        )
        high = lax.ppermute(lax.slice_in_dim(block, 0, width, axis=dim), axis, backward)
        block = jnp.concatenate([low, block, high], axis=dim)
    return block


def shards(
    sources,
    self_terms,
    near_tiles,
    near_cols,
    near_count,
    far_cols,
    basis_left,
    basis_right,
    couplings,
):
    local_blocks = near_cols.shape[0]
    block_size = near_tiles.shape[-1]
    columns = sources.shape[1]
    all_blocks = local_blocks * lax.axis_size("store")
    all_panels = all_blocks * block_size
    first_block = lax.axis_index("store") * local_blocks
    global_rows = first_block + jnp.arange(local_blocks, dtype=jnp.int32)
    relative = (near_cols - global_rows[:, None] + REACH) % all_blocks - REACH
    extended = jnp.arange(local_blocks, dtype=jnp.int32)[:, None] + REACH + relative
    highest = jnp.max(near_count)
    diagonal = self_terms.reshape(2, local_blocks, block_size)

    def far_rows(inputs):
        coeffs = jnp.einsum(
            "bpr,kbps->kbrs", basis_right, inputs, preferred_element_type=jnp.float32
        ).astype(jnp.bfloat16)
        gathered = lax.all_gather(coeffs, "store", axis=1, tiled=True)
        picked = gathered[:, far_cols]
        picked = jnp.broadcast_to(picked, (2,) + picked.shape[1:])
        reduced = jnp.einsum(
            "obfrq,obfqs->obrs", couplings, picked, preferred_element_type=jnp.float32
        ).astype(jnp.bfloat16)
        return jnp.einsum(
            "bpr,obrs->obps", basis_left, reduced, preferred_element_type=jnp.float32
        ).astype(jnp.bfloat16)

    def operate(inputs):
        padded = padded_2(inputs, (("store", 1),), REACH)

        def add_slot(position, accum):
            which = lax.dynamic_index_in_dim(extended, position, 1, keepdims=False)
            taken = jnp.take(padded, which, axis=1)
            taken = jnp.broadcast_to(taken, (2,) + taken.shape[1:])
            tiles_now = lax.dynamic_index_in_dim(near_tiles, position, 2, keepdims=False)
            product = jnp.einsum(
                "obpq,obqs->obps", tiles_now, taken, preferred_element_type=jnp.float32
            )
            weight = (position < near_count).astype(jnp.float32)
            return accum + product * weight[None, :, None, None]

        start = jnp.zeros((2, local_blocks, block_size, columns), jnp.float32)
        near_part = lax.fori_loop(0, highest, add_slot, start)
        far_part = far_rows(inputs)
        return (
            near_part
            + diagonal[..., None] * inputs.astype(jnp.float32)
            + far_part.astype(jnp.float32)
        )

    source_f = sources.astype(jnp.float32).reshape(local_blocks, block_size, columns)
    scale_sq = lax.psum(jnp.sum(source_f * source_f, axis=(0, 1)), "store") / all_panels
    first_vec = (source_f / jnp.sqrt(scale_sq + EPSILON)).astype(jnp.bfloat16)
    image_one = operate(first_vec[None])
    first_f = first_vec.astype(jnp.float32)
    heights = lax.psum(jnp.sum(first_f[None] * image_one, axis=(1, 2)), "store") / all_panels
    remain = image_one - heights[:, None, None, :] * first_f[None]
    spread = lax.psum(jnp.sum(remain * remain, axis=(1, 2)), "store") / all_panels
    norms = jnp.sqrt(spread + EPSILON)
    second_vec = (remain / norms[:, None, None, :]).astype(jnp.bfloat16)
    image_two = operate(second_vec)
    return (image_two.reshape(2, local_blocks * block_size, columns), heights, norms)


def solution(mesh):
    placed = (
        P(("groups", "store"), None),
        P(None, "store"),
        P(None, "store", None, None, None),
        P("store", None),
        P("store"),
        P("store", None),
        P("store", None, None),
        P("store", None, None),
        P(None, "store", None, None, None),
    )
    return jax.shard_map(
        shards,
        mesh=mesh,
        in_specs=placed,
        out_specs=(P(None, ("groups", "store"), None), P("groups", None), P("groups", None)),
        check_vma=False,
    )
```

profile of v0, /device:TPU:1, one launch (start us, length us, event | category | flops | bytes accessed | tf_op | source)
XLA Modules:
  0.0 223.8 jit_solution(12892225822094660299)
XLA Ops:
  9.6 30.6 %psum.21 = f32[512]{0:T(512)S(1)} all-reduce(f32[512]{0:T(512)S(1)} %multiply_reduce_fusion.2), channel_id=1, replica_groups=mesh['groups'=2,'store'=16] {'store'}, use_global_device_ids=true, to_apply=%region_2.3 | all-reduce | flops 512 | bytes 4096 | tf_op jit(solution)/shard_map/psum | solution.py:87
  41.5 3.4 %collective-permute-start.1 = (bf16[1,2,256,512]{3,2,1,0:T(8,128)(2,1)S(1)}, bf16[1,2,256,512]{3,2,1,0:T(8,128)(2,1)S(1)}, u32[]{:S(2)}, u32[]{:S(2)}) collective-permute-start(bf16[1,2,256,512]{3,2,1,0:T(8,128)(2,1)S(1)} %divide_convert_fusion.2), channel_id=1, source_target_pairs={{1,0},{2,1},{3,2},{4,3},{5,4},{6,5},{7,6},{8,7},{9,8},{10,9},{11,1... | collective-permute-start | bytes 1572872 | tf_op jit(solution)/shard_map/ppermute | solution.py:21
  47.0 3.5 %copy.36 = bf16[2,2,5,256,256]{4,3,1,0,2:T(8,128)(2,1)} copy(bf16[2,2,5,256,256]{4,3,2,1,0:T(8,128)(2,1)} %param.15) | data formatting | bytes 5242880 | tf_op jit(solution)/shard_map/while | solution.py:78
  52.4 3.3 %collective-permute-done.1 = bf16[1,2,256,512]{3,2,1,0:T(8,128)(2,1)S(1)} collective-permute-done((bf16[1,2,256,512]{3,2,1,0:T(8,128)(2,1)S(1)}, bf16[1,2,256,512]{3,2,1,0:T(8,128)(2,1)S(1)}, u32[]{:S(2)}, u32[]{:S(2)}) %collective-permute-start.1) | collective-permute-done | bytes 524320 | tf_op jit(solution)/shard_map/ppermute | solution.py:21
  57.3 18.7 %while.20 = (s32[]{:T(128)}, f32[2,2,256,512]{3,2,1,0:T(8,128)S(1)}, s32[]{:T(128)}, bf16[2,2,5,256,256]{4,3,1,0,2:T(8,128)(2,1)}, s32[2,5]{0,1:T(8,128)S(1)}, /...) while((s32[]{:T(128)}, f32[2,2,256,512]{3,2,1,0:T(8,128)S(1)}, ...), condition=%wide.region_4.5_spmd, body=%wide.region_3.4_spmd.sunk | while | flops 269747232 | bytes 7344335 | solution.py:78
  58.1 2.0 gather_fusion
  60.2 1.6 multiply_add_fusion.4
  62.5 2.0 gather_fusion
  67.0 2.0 gather_fusion
  71.4 2.1 gather_fusion
  76.0 10.4 %all-gather.3.cloned.1.call-done = bf16[1,32,32,512]{3,2,0,1:T(8,128)(2,1)} async-done(((bf16[1,2,32,512]{3,2,0,1:T(8,128)(2,1)}), bf16[1,32,32,512]{3,2,0,1:T(8,128)(2,1)}) %all-gather.3.cloned.1.call-update) | async-done | bytes 1048592 | tf_op jit(solution)/shard_map/all_gather | solution.py:53
  86.3 2.5 %gather_fusion.2 = bf16[12,32,512]{2,1,0:T(8,128)(2,1)} fusion(bf16[32,32,512]{2,1,0:T(8,128)(2,1)} %bitcast.109, s32[1024]{0:T(1024)S(1)} %pad_clamp_fusion.2), kind=kCustom, calls=%fused_computation.2 | custom fusion | bytes 786480 | tf_op jit(solution)/shard_map/gather | solution.py:54
  88.9 3.7 %multiply_reduce_fusion.1 = (f32[2,512]{1,0:T(2,128)S(1)}, f32[2,2,256,512]{3,2,0,1:T(8,128)}) fusion(f32[2,256,512]{2,1,0:T(8,128)} %get-tuple-element.155, bf16[2,256,32]{1,2,0:T(8,128)(2,1)S(1)} %copy-done, bf16[2,6,32,512]{3,2,1,0:T(8,128)(2,1)} %bitcast.108, bf16[2,2,6,32,32]{4,3,2,1,0:T(8,128)(2,1)S(1)} %copy-done.3, f32[2,2,256]{2,0,1:T(2,128)S(1)} %bitcast.112, ...), kind=kOutput, calls=%fused_computation.32 | convolution fusion | flops 62454784 | bytes 5726208 | tf_op jit(solution)/shard_map/bpr,obrs->obps/dot_general | solution.py:59
  92.6 29.2 %psum.22 = f32[2,512]{1,0:T(2,128)S(1)} all-reduce(f32[2,512]{1,0:T(2,128)S(1)} %get-tuple-element.157), channel_id=1, replica_groups=mesh['groups'=2,'store'=16] {'store'}, use_global_device_ids=true, to_apply=%region_6.7 | all-reduce | flops 1024 | bytes 8192 | tf_op jit(solution)/shard_map/psum | solution.py:91
  121.9 2.0 multiply_reduce_fusion
  123.9 31.6 %psum.23 = f32[2,512]{1,0:T(2,128)S(1)} all-reduce(f32[2,512]{1,0:T(2,128)S(1)} %multiply_reduce_fusion), channel_id=1, replica_groups=mesh['groups'=2,'store'=16] {'store'}, use_global_device_ids=true, to_apply=%region_8.9 | all-reduce | flops 1024 | bytes 8192 | tf_op jit(solution)/shard_map/psum | solution.py:93
  157.6 2.2 fusion.12
  159.8 20.1 %collective-permute-done.2 = bf16[2,2,256,512]{3,2,0,1:T(8,128)(2,1)S(1)} collective-permute-done((bf16[2,2,256,512]{3,2,0,1:T(8,128)(2,1)}, bf16[2,2,256,512]{3,2,0,1:T(8,128)(2,1)S(1)}, u32[]{:S(2)}, u32[]{:S(2)}) %collective-permute-start.2) | collective-permute-done | bytes 1048608 | tf_op jit(solution)/shard_map/ppermute | solution.py:18
  179.9 4.1 %collective-permute-done.3 = bf16[2,2,256,512]{3,2,0,1:T(8,128)(2,1)S(1)} collective-permute-done((bf16[2,2,256,512]{3,2,0,1:T(8,128)(2,1)}, bf16[2,2,256,512]{3,2,0,1:T(8,128)(2,1)S(1)}, u32[]{:S(2)}, u32[]{:S(2)}) %collective-permute-start.3) | collective-permute-done | bytes 1048608 | tf_op jit(solution)/shard_map/ppermute | solution.py:21
  185.5 1.8 copy.37
  187.6 20.6 %while.21 = (s32[]{:T(128)}, f32[2,2,256,512]{3,2,1,0:T(8,128)S(1)}, s32[]{:T(128)}, bf16[2,2,5,256,256]{4,3,1,0,2:T(8,128)(2,1)}, s32[2,5]{0,1:T(8,128)S(1)}, /...) while((s32[]{:T(128)}, f32[2,2,256,512]{3,2,1,0:T(8,128)S(1)}, ...), condition=%wide.region_10.11_spmd, body=%wide.region_9.10_spmd.sunk | while | flops 270009376 | bytes 7868623 | solution.py:78
  188.3 2.5 %gather_fusion.1 = bf16[2,2,256,512]{3,2,1,0:T(8,128)(2,1)S(1)} fusion(bf16[2,6,256,512]{3,2,1,0:T(8,128)(2,1)} %get-tuple-element.312, s32[1024]{0:T(1024)S(1)} %pad_clamp_fusion.6), kind=kCustom, calls=%fused_computation.1.clone.1 | custom fusion | bytes 2097160 | tf_op jit(solution)/shard_map/while/body/jit(_take)/gather | solution.py:68
  190.8 1.7 multiply_add_fusion.5
  193.2 2.5 %gather_fusion.1 = bf16[2,2,256,512]{3,2,1,0:T(8,128)(2,1)S(1)} fusion(bf16[2,6,256,512]{3,2,1,0:T(8,128)(2,1)} %get-tuple-element.312, s32[1024]{0:T(1024)S(1)} %pad_clamp_fusion.6), kind=kCustom, calls=%fused_computation.1.clone.1 | custom fusion | bytes 2097160 | tf_op jit(solution)/shard_map/while/body/jit(_take)/gather | solution.py:68
  195.8 1.7 multiply_add_fusion.5
  198.2 2.6 %gather_fusion.1 = bf16[2,2,256,512]{3,2,1,0:T(8,128)(2,1)S(1)} fusion(bf16[2,6,256,512]{3,2,1,0:T(8,128)(2,1)} %get-tuple-element.312, s32[1024]{0:T(1024)S(1)} %pad_clamp_fusion.6), kind=kCustom, calls=%fused_computation.1.clone.1 | custom fusion | bytes 2097160 | tf_op jit(solution)/shard_map/while/body/jit(_take)/gather | solution.py:68
  200.8 1.7 multiply_add_fusion.5
  203.2 2.5 %gather_fusion.1 = bf16[2,2,256,512]{3,2,1,0:T(8,128)(2,1)S(1)} fusion(bf16[2,6,256,512]{3,2,1,0:T(8,128)(2,1)} %get-tuple-element.312, s32[1024]{0:T(1024)S(1)} %pad_clamp_fusion.6), kind=kCustom, calls=%fused_computation.1.clone.1 | custom fusion | bytes 2097160 | tf_op jit(solution)/shard_map/while/body/jit(_take)/gather | solution.py:68
  205.8 1.7 multiply_add_fusion.5
  208.2 2.2 gather_fusion.3
  210.4 3.5 %bitcast_add_fusion = f32[2,2,256,512]{3,2,0,1:T(8,128)} fusion(f32[2,2,256,512]{3,2,1,0:T(8,128)S(1)} %get-tuple-element.80, bf16[2,2,256,512]{3,2,0,1:T(8,128)(2,1)} %divide_convert_fusion, f32[2,2,256]{2,0,1:T(2,128)S(1)} %bitcast.113, bf16[2,6,2,32,512]{4,3,2,1,0:T(8,128)(2,1)S(1)} %bitcast.106, bf16[2,2,6,32,32]{4,3,2,1,0:T(8,128)(2,1)S(1)} %copy-done.3, ...), kind=kOutput, calls=%fused_computation.25 | convolution fusion | flops 61931520 | bytes 6115328 | tf_op jit(solution)/shard_map/bpr,obrs->obps/dot_general | solution.py:59
  213.9 3.1 %copy.41 = f32[2,2,256,512]{3,2,1,0:T(8,128)} copy(f32[2,2,256,512]{3,2,0,1:T(8,128)} %bitcast_add_fusion) | data formatting | bytes 4194304 | tf_op jit(solution)/shard_map/add | solution.py:81
  (82 shorter events, 18.5 us)
Async XLA Ops:
  7.2 81.7 %copy-start = (bf16[2,256,32]{1,2,0:T(8,128)(2,1)S(1)}, bf16[2,256,32]{1,2,0:T(8,128)(2,1)}, u32[]{:S(2)}) copy-start(bf16[2,256,32]{1,2,0:T(8,128)(2,1)} %param.19) | copy-start | bytes 98308
  7.2 79.2 %all-gather.3.cloned.1.call-start = ((), (), s32[]{:S(2)}) async-start(), calls=%async_computation | async-start | bytes 1114112 | tf_op jit(solution)/shard_map/all_gather | solution.py:53
  40.2 5.8 %copy-start.4 = (bf16[2,256,32]{1,2,0:T(8,128)(2,1)S(1)}, bf16[2,256,32]{1,2,0:T(8,128)(2,1)}, u32[]{:S(2)}) copy-start(bf16[2,256,32]{1,2,0:T(8,128)(2,1)} %param.20) | copy-start | bytes 98308
  40.2 6.7 %copy-start.9 = (s32[2,6]{1,0:T(2,128)S(1)}, s32[2,6]{1,0:T(2,128)}, u32[]{:S(2)}) copy-start(s32[2,6]{1,0:T(2,128)} %param.18) | copy-start | bytes 148
  40.2 6.7 %copy-start.8 = (s32[2,5]{1,0:T(2,128)S(1)}, s32[2,5]{1,0:T(2,128)}, u32[]{:S(2)}) copy-start(s32[2,5]{1,0:T(2,128)} %param.16) | copy-start | bytes 124
  40.3 12.0 %collective-permute-start = (bf16[1,2,256,512]{3,2,1,0:T(8,128)(2,1)S(1)}, bf16[1,2,256,512]{3,2,1,0:T(8,128)(2,1)S(1)}, u32[]{:S(2)}, u32[]{:S(2)}) collective-permute-start(bf16[1,2,256,512]{3,2,1,0:T(8,128)(2,1)S(1)} %divide_convert_fusion.2), channel_id=1, source_target_pairs={{0,1},{1,2},{2,3},{3,4},{4,5},{5,6},{6,7},{7,8},{8,9},{9,10},{10,1... | collective-permute-start | bytes 1572872 | tf_op jit(solution)/shard_map/ppermute | solution.py:18
  41.5 14.2 %collective-permute-start.1 = (bf16[1,2,256,512]{3,2,1,0:T(8,128)(2,1)S(1)}, bf16[1,2,256,512]{3,2,1,0:T(8,128)(2,1)S(1)}, u32[]{:S(2)}, u32[]{:S(2)}) collective-permute-start(bf16[1,2,256,512]{3,2,1,0:T(8,128)(2,1)S(1)} %divide_convert_fusion.2), channel_id=1, source_target_pairs={{1,0},{2,1},{3,2},{4,3},{5,4},{6,5},{7,6},{8,7},{9,8},{10,9},{11,1... | collective-permute-start | bytes 1572872 | tf_op jit(solution)/shard_map/ppermute | solution.py:21
  46.9 161.3 %all-gather.5.cloned.1.call-start = ((), (), s32[]{:S(2)}) async-start(), calls=%async_computation.1 | async-start | bytes 2228224 | tf_op jit(solution)/shard_map/all_gather | solution.py:53
  47.0 3.6 %copy-start.10 = (s32[2]{0:T(128)S(1)}, s32[2]{0:T(128)}, u32[]{:S(2)}) copy-start(s32[2]{0:T(128)} %param.17) | copy-start | bytes 28
  57.3 31.6 %copy-start.3 = (bf16[2,2,6,32,32]{4,3,2,1,0:T(8,128)(2,1)S(1)}, bf16[2,2,6,32,32]{4,3,2,1,0:T(8,128)(2,1)}, u32[]{:S(2)}) copy-start(bf16[2,2,6,32,32]{4,3,2,1,0:T(8,128)(2,1)} %param.21) | copy-start | bytes 147460
  57.3 31.6 %copy-start.7 = (f32[2,512]{1,0:T(2,128)S(1)}, f32[2,512]{1,0:T(2,128)}, u32[]{:S(2)}) copy-start(f32[2,512]{1,0:T(2,128)} %param.14) | copy-start | bytes 12292
  88.9 33.0 %copy-start.2 = (f32[2,256,512]{2,1,0:T(8,128)S(1)}, f32[2,256,512]{2,1,0:T(8,128)}, u32[]{:S(2)}) copy-start(f32[2,256,512]{2,1,0:T(8,128)} %get-tuple-element.155) | copy-start | bytes 3145732
  92.6 62.8 %copy-start.1 = (f32[2,2,256,512]{3,2,0,1:T(8,128)S(1)}, f32[2,2,256,512]{3,2,0,1:T(8,128)}, u32[]{:S(2)}) copy-start(f32[2,2,256,512]{3,2,0,1:T(8,128)} %get-tuple-element.158) | copy-start | bytes 6291460
  121.9 35.0 %copy-start.5 = (f32[2,512]{1,0:T(2,128)}, f32[2,512]{1,0:T(2,128)S(1)}, u32[]{:S(2)}) copy-start(f32[2,512]{1,0:T(2,128)S(1)} %broadcast_multiply_fusion) | copy-start | bytes 12292
  155.5 1.4 copy-start.6
  156.9 23.0 %collective-permute-start.2 = (bf16[2,2,256,512]{3,2,0,1:T(8,128)(2,1)}, bf16[2,2,256,512]{3,2,0,1:T(8,128)(2,1)S(1)}, u32[]{:S(2)}, u32[]{:S(2)}) collective-permute-start(bf16[2,2,256,512]{3,2,0,1:T(8,128)(2,1)} %divide_convert_fusion), channel_id=1, source_target_pairs={{0,1},{1,2},{2,3},{3,4},{4,5},{5,6},{6,7},{7,8},{8,9},{9,10},{10,1... | collective-permute-start | bytes 3145736 | tf_op jit(solution)/shard_map/ppermute | solution.py:18
  156.9 27.1 %collective-permute-start.3 = (bf16[2,2,256,512]{3,2,0,1:T(8,128)(2,1)}, bf16[2,2,256,512]{3,2,0,1:T(8,128)(2,1)S(1)}, u32[]{:S(2)}, u32[]{:S(2)}) collective-permute-start(bf16[2,2,256,512]{3,2,0,1:T(8,128)(2,1)} %divide_convert_fusion), channel_id=1, source_target_pairs={{1,0},{2,1},{3,2},{4,3},{5,4},{6,5},{7,6},{8,7},{9,8},{10,9},{11,1... | collective-permute-start | bytes 3145736 | tf_op jit(solution)/shard_map/ppermute | solution.py:21
Sparse Core Ops, SparseCore 0:
  47.0 39.3 all-gather.2
  159.9 47.5 all-gather.4
where the time goes:
time: 225 us; the launch traced here: 224 us
  blocking collectives  91.4 us (41%)
  waiting for transfers between devices  39 us (17%)
  local copies, waits for them, and re-layouts  32.1 us (14%)
  matrix products  23.4 us (10%)
  between operations  14.2 us (6%)
  other arithmetic  11.2 us (5%)
  loops' own time  7.21 us (3%)
  starting transfers between devices  5.3 us (2%)
    psum x1, blocking collectives, shards(): lax.psum(jnp.sum(remain * remain, axis=(1, 2)), 'store') / all_panels  31.6 us
    psum x1, blocking collectives, shards(): lax.psum(jnp.sum(source_f * source_f, axis=(0, 1)), 'store') / all_panels  30.6 us
    psum x1, blocking collectives, shards(): lax.psum(jnp.sum(first_f[None] * image_one, axis=(1, 2)), 'store')  29.2 us
    ppermute x2, waiting for transfers between devices, padded_2(): lax.ppermute(lax.slice_in_dim(block, block.shape[dim] - width, None, axis...  21.1 us
    gather x8, local copies, waits for them, and re-layouts, add_slot(): taken = jnp.take(padded, which, axis=1)  18.2 us
    dot_general x8, matrix products, add_slot(): jnp.einsum('obpq,obqs->obps', tiles_now, taken, preferred_element_type=jn...  13.2 us
    all_gather x2, waiting for transfers between devices, far_rows(): gathered = lax.all_gather(coeffs, 'store', axis=1, tiled=True)  10.4 us
    ppermute x2, waiting for transfers between devices, padded_2(): lax.ppermute(lax.slice_in_dim(block, 0, width, axis=dim), axis, backward)  7.45 us
  transfers between devices with their start and end apart: 6, of which 5 were waited for; matrix products, arithmetic and copies ran while one was open for 20% of the time, Pallas kernels for 0%

commit v1 on v0

v1 whole, which is shorter than its diff:
```python
import functools

import jax
import jax.numpy as jnp
from jax import lax
from jax.experimental import pallas as pl
from jax.experimental.pallas import tpu as pltpu
from jax.sharding import PartitionSpec as P

REACH = 2
EPSILON = 1e-06
CHUNK = 256
CORES = 2
TINY = 1e-30
MESH = pl.DeviceIdType.MESH
F32 = jnp.float32
BF16 = jnp.bfloat16


def kernel(
    devices,
    cols_ref,
    count_ref,
    far_ref,
    src_ref,
    self_ref,
    tiles_ref,
    left_ref,
    right_ref,
    coup_ref,
    out_ref,
    heights_ref,
    norms_ref,
    w_ref,
    g_ref,
    self_col,
    u1,
    u2,
    z1,
    z2,
    zsel,
    y_ref,
    stats,
    h1_send,
    h1_recv,
    h2_send,
    h2_recv,
    z1_send,
    z1_fsend,
    z1_recv,
    z2_send,
    z2_fsend,
    z2_recv,
    st_send,
    st_recv,
):
    me = lax.axis_index("store")
    chips = devices // CORES
    chip = me // CORES
    core = me % CORES
    partner = chip * CORES + (1 - core)
    right = (me + 1) % devices
    left = (me + devices - 1) % devices
    local = tiles_ref.shape[1]
    near = tiles_ref.shape[2]
    size = tiles_ref.shape[3]
    far = coup_ref.shape[2]
    rank = coup_ref.shape[3]
    rows = local * size
    width = u1.shape[2]
    chunks = u1.shape[0]
    blocks = devices * local
    panels = blocks * size

    def remote(src, dst, send, recv, peer):
        return pltpu.make_async_remote_copy(
            src_ref=src,
            dst_ref=dst,
            send_sem=send,
            recv_sem=recv,
            device_id={"store": peer},
            device_id_type=MESH,
        )

    barrier = pltpu.get_barrier_semaphore()

    @pl.loop(1, devices)
    def _(t):
        pl.semaphore_signal(
            barrier, inc=1, device_id={"store": (me + t) % devices}, device_id_type=MESH
        )

    pl.semaphore_wait(barrier, devices - 1)

    def halo(field, c, send, recv):
        own = field.at[pl.ds(rows, rows)]
        return (
            remote(own, field.at[pl.ds(0, rows)], send.at[c, 0], recv.at[c, 0], right),
            remote(own, field.at[pl.ds(2 * rows, rows)], send.at[c, 1], recv.at[c, 1], left),
        )

    def coeff_copy(z, c, send, recv, source, peer):
        part = z[c].at[pl.ds(source * local, local)]
        return remote(part, part, send, recv.at[c, source], peer)

    def coeff_start(z, c, send, recv):
        coeff_copy(z, c, send.at[c, 0], recv, me, partner).start()

        @pl.loop(1, chips)
        def _(t):
            peer = ((chip + t) % chips) * CORES + core
            coeff_copy(z, c, send.at[c, t], recv, me, peer).start()

    def coeff_forward(z, c, fsend, recv):
        @pl.loop(1, chips)
        def _(t):
            source = ((chip + chips - t) % chips) * CORES + core
            copy = coeff_copy(z, c, fsend.at[c, t], recv, source, partner)
            copy.wait_recv()
            copy.start()

    def coeff_wait(z, c, fsend, recv):
        coeff_copy(z, c, fsend.at[c, 0], recv, partner, partner).wait_recv()

        @pl.loop(1, chips)
        def _(t):
            source = ((chip + chips - t) % chips) * CORES + (1 - core)
            coeff_copy(z, c, fsend.at[c, t], recv, source, partner).wait_recv()

    def coeff_drain(z, c, send, fsend, recv):
        coeff_copy(z, c, send.at[c, 0], recv, me, partner).wait_send()

        @pl.loop(1, chips)
        def _(t):
            coeff_copy(z, c, send.at[c, t], recv, me, partner).wait_send()
            coeff_copy(z, c, fsend.at[c, t], recv, me, partner).wait_send()

    def stat_copy(c, source, peer, t):
        part = stats.at[c, source]
        return remote(part, part, st_send.at[c, t], st_recv.at[c, source], peer)

    def to_coeffs(r, values):
        return lax.dot_general(
            right_ref[r], values, (((0,), (0,)), ((), ())), preferred_element_type=F32
        ).astype(BF16)

    for c in range(chunks):
        cut = pl.ds(c * width, width)
        u1[c, pl.ds(rows, rows)] = src_ref[:, cut]
        for copy in halo(u1.at[c], c, h1_send, h1_recv):
            copy.start()
        for r in range(local):
            z1[c][me * local + r] = to_coeffs(r, src_ref[pl.ds(r * size, size), cut])
        coeff_start(z1, c, z1_send, z1_recv)

    for r in range(local):
        row = me * local + r
        for d in range(near):
            target = (row + d - REACH + blocks) % blocks
            slot = jnp.int32(0)
            for k in range(1, near):
                slot = jnp.where(cols_ref[r, k] == target, k, slot)
            live = (slot < count_ref[r]).astype(F32).astype(BF16)
            for o in range(2):
                w_ref[o, r, :, pl.ds(d * size, size)] = tiles_ref[o, r, slot] * live
        for o in range(2):
            parts = [
                lax.dot_general(
                    coup_ref[o, r, k],
                    left_ref[r],
                    (((0,), (1,)), ((), ())),
                    preferred_element_type=F32,
                )
                for k in range(far)
            ]
            parts.append(jnp.zeros((g_ref.shape[3] - far * rank, size), F32))
            g_ref[o, r] = jnp.concatenate(parts, axis=0).T.astype(BF16)
        diag = lax.broadcasted_iota(jnp.int32, (size, size), 0) == lax.broadcasted_iota(
            jnp.int32, (size, size), 1
        )
        for o in range(2):
            line = self_ref[pl.ds(o, 1), pl.ds(r * size, size)]
            self_col[o, pl.ds(r * size, size)] = jnp.sum(
                jnp.where(diag, line, 0.0), axis=1, keepdims=True
            )
    zsel[...] = jnp.zeros_like(zsel)

    def product(o, r, field, z, c, offset):
        for k in range(far):
            zsel[r, pl.ds(k * rank, rank)] = z[c][far_ref[r, k], pl.ds(offset, rank)]
        total = jnp.dot(
            w_ref[o, r],
            field[pl.ds(r * size, near * size)],
            preferred_element_type=F32,
        )
        total += jnp.dot(g_ref[o, r], zsel[r], preferred_element_type=F32)
        own = field[pl.ds(rows + r * size, size)].astype(F32)
        return total + self_col[o, pl.ds(r * size, size)] * own, own

    def first(c):
        coeff_forward(z1, c, z1_fsend, z1_recv)
        coeff_wait(z1, c, z1_fsend, z1_recv)
        for copy in halo(u1.at[c], c, h1_send, h1_recv):
            copy.wait_recv()
        q = jnp.zeros((1, width), F32)
        p = [jnp.zeros((1, width), F32) for _ in range(2)]
        for r in range(local):
            for o in range(2):
                value, own = product(o, r, u1.at[c], z1, c, 0)
                y_ref[c, o, pl.ds(r * size, size)] = value
                p[o] += jnp.sum(value * own, axis=0, keepdims=True)
                if o == 0:
                    q += jnp.sum(own * own, axis=0, keepdims=True)
        h = [p[o] / jnp.maximum(q, TINY) for o in range(2)]
        rest = []
        for o in range(2):
            own = src_ref[:, pl.ds(c * width, width)].astype(F32)
            rem = y_ref[c, o] - h[o] * own
            rest.append(jnp.sum(rem * rem, axis=0, keepdims=True))
        zero = jnp.zeros((1, width), F32)
        stats[c, me] = jnp.concatenate([q, *p, *h, *rest, zero], axis=0)

        @pl.loop(1, devices)
        def _(t):
            stat_copy(c, me, (me + t) % devices, t).start()

    def second(c):
        @pl.loop(1, devices)
        def _(t):
            stat_copy(c, (me + devices - t) % devices, me, t).wait_recv()

        cut = pl.ds(c * width, width)
        every = stats[c]
        sums = jnp.sum(every, axis=0)
        scale = sums[0:1] / panels
        inv = 1.0 / jnp.sqrt(scale + EPSILON)
        own = src_ref[:, cut].astype(F32)
        root = jnp.sqrt(every[:, 0:1])
        for o in range(2):
            h = sums[1 + o : 2 + o] * inv * inv / panels
            off = (every[:, 3 + o : 4 + o] - h[None]) * root
            spread = (sums[5 + o : 6 + o] + jnp.sum(off * off, axis=0)) * inv * inv / panels
            norm = jnp.sqrt(spread + EPSILON)
            heights_ref[pl.ds(o, 1), cut] = h
            norms_ref[pl.ds(o, 1), cut] = norm
            value = ((y_ref[c, o] - h * own) * (inv / norm)).astype(BF16)
            u2[c, o, pl.ds(rows, rows)] = value
            for copy in halo(u2.at[c, o], 2 * c + o, h2_send, h2_recv):
                copy.start()
            for r in range(local):
                z2[c][me * local + r, pl.ds(o * rank, rank)] = to_coeffs(
                    r, value[r * size : (r + 1) * size]
                )
        coeff_start(z2, c, z2_send, z2_recv)

    def third(c):
        coeff_forward(z2, c, z2_fsend, z2_recv)
        coeff_wait(z2, c, z2_fsend, z2_recv)
        for o in range(2):
            for copy in halo(u2.at[c, o], 2 * c + o, h2_send, h2_recv):
                copy.wait_recv()
            for r in range(local):
                value, _ = product(o, r, u2.at[c, o], z2, c, o * rank)
                out_ref[o, pl.ds(r * size, size), pl.ds(c * width, width)] = value

    for c in range(chunks):
        first(c)
        if c >= 1:
            second(c - 1)
    second(chunks - 1)
    for c in range(chunks):
        third(c)

    for c in range(chunks):
        for copy in halo(u1.at[c], c, h1_send, h1_recv):
            copy.wait_send()
        for o in range(2):
            for copy in halo(u2.at[c, o], 2 * c + o, h2_send, h2_recv):
                copy.wait_send()
        coeff_drain(z1, c, z1_send, z1_fsend, z1_recv)
        coeff_drain(z2, c, z2_send, z2_fsend, z2_recv)

        @pl.loop(1, devices)
        def _(t):
            stat_copy(c, me, partner, t).wait_send()


def shards(
    devices,
    sources,
    self_terms,
    near_tiles,
    near_cols,
    near_count,
    far_cols,
    basis_left,
    basis_right,
    couplings,
):
    rows, columns = sources.shape
    local, near, size = near_tiles.shape[1:4]
    far, rank = couplings.shape[2:4]
    blocks = devices * local
    chunks = columns // CHUNK
    chips = devices // CORES
    depth = -(-far * rank // 128) * 128
    dma = pltpu.SemaphoreType.DMA
    smem = pl.BlockSpec(memory_space=pltpu.SMEM)
    vmem = pl.BlockSpec(memory_space=pltpu.VMEM)
    return pl.pallas_call(
        functools.partial(kernel, devices),
        out_shape=(
            jax.ShapeDtypeStruct((2, rows, columns), F32),
            jax.ShapeDtypeStruct((2, columns), F32),
            jax.ShapeDtypeStruct((2, columns), F32),
        ),
        in_specs=[smem] * 3 + [vmem] * 6,
        out_specs=(vmem,) * 3,
        scratch_shapes=[
            pltpu.VMEM((2, local, size, near * size), BF16),
            pltpu.VMEM((2, local, size, depth), BF16),
            pltpu.VMEM((2, rows, 1), F32),
            pltpu.VMEM((chunks, 3 * rows, CHUNK), BF16),
            pltpu.VMEM((chunks, 2, 3 * rows, CHUNK), BF16),
            [pltpu.VMEM((blocks, rank, CHUNK), BF16)] * chunks,
            [pltpu.VMEM((blocks, 2 * rank, CHUNK), BF16)] * chunks,
            pltpu.VMEM((local, depth, CHUNK), BF16),
            pltpu.VMEM((chunks, 2, rows, CHUNK), F32),
            pltpu.VMEM((chunks, devices, 8, CHUNK), F32),
            dma((chunks, 2)),
            dma((chunks, 2)),
            dma((2 * chunks, 2)),
            dma((2 * chunks, 2)),
            dma((chunks, chips)),
            dma((chunks, chips)),
            dma((chunks, devices)),
            dma((chunks, chips)),
            dma((chunks, chips)),
            dma((chunks, devices)),
            dma((chunks, devices)),
            dma((chunks, devices)),
        ],
        compiler_params=pltpu.CompilerParams(
            collective_id=0, has_side_effects=True, vmem_limit_bytes=56 * 1024 * 1024
        ),
    )(
        near_cols,
        near_count,
        far_cols,
        sources,
        self_terms,
        near_tiles,
        basis_left,
        basis_right,
        couplings,
    )


def solution(mesh):
    placed = (
        P(("groups", "store"), None),
        P(None, "store"),
        P(None, "store", None, None, None),
        P("store", None),
        P("store"),
        P("store", None),
        P("store", None, None),
        P("store", None, None),
        P(None, "store", None, None, None),
    )
    return jax.shard_map(
        functools.partial(shards, mesh.shape["store"]),
        mesh=mesh,
        in_specs=placed,
        out_specs=(P(None, ("groups", "store"), None), P("groups", None), P("groups", None)),
        check_vma=False,
    )
```

time: 225 us -> 81.7 us (0.36)
  blocking collectives: 91.4 us -> 0 us
  Pallas kernels: 0 us -> 73.4 us
  waiting for transfers between devices: 39 us -> 0 us
  local copies, waits for them, and re-layouts: 32.1 us -> 7.32 us
  matrix products: 23.4 us -> 0 us
  between operations: 14.2 us -> 0.66 us
  other arithmetic: 11.2 us -> 0 us
  loops' own time: 7.21 us -> 0 us
  starting transfers between devices: 5.3 us -> 0 us
    psum x3 -> x0, blocking collectives: 91.4 us -> none  [the longest x1 31.6 us: shards(): lax.psum(jnp.sum(remain * remain, axis=(1, 2)), 'store') / all_panels]
    pallas_call x0 -> x1, Pallas kernels: none -> 73.4 us  [shards(): pl.pallas_call(functools.partial(kernel, devices), out_shape=(jax.ShapeDt...]
    ppermute x4 -> x0, waiting for transfers between devices: 28.6 us -> none  [the longest x2 21.1 us: padded_2(): lax.ppermute(lax.slice_in_dim(block, block.shape[dim] - width, None, axis...]
    dot_general x12 -> x0, matrix products: 23.4 us -> none  [the longest x8 13.2 us: add_slot(): jnp.einsum('obpq,obqs->obps', tiles_now, taken, preferred_element_type=jn...]
    gather x10 -> x0, local copies, waits for them, and re-layouts: 22.9 us -> none  [the longest x8 18.2 us: add_slot(): taken = jnp.take(padded, which, axis=1)]
    all_gather x2 -> x0, waiting for transfers between devices: 10.4 us -> none  [far_rows(): gathered = lax.all_gather(coeffs, 'store', axis=1, tiled=True)]
    another operation x2 -> x0, loops' own time: 7.21 us -> none  [operate(): near_part = lax.fori_loop(0, highest, add_slot, start)]
    unnamed x23 -> x9, local copies, waits for them, and re-layouts: 0.15 us -> 7.32 us
  transfers between devices with their start and end apart: 6 -> 0, of which waited for: 5 -> 0; matrix products, arithmetic and copies ran while one was open for 20% -> 0% of each run, Pallas kernels for 0% -> 0%
where the time goes in v1:
time: 81.7 us; the launch traced here: 81.4 us
  Pallas kernels  73.4 us (90%)
  local copies, waits for them, and re-layouts  7.32 us (9%)
    pallas_call x1, Pallas kernels, shards(): pl.pallas_call(functools.partial(kernel, devices), out_shape=(jax.ShapeDt...  73.4 us
    unnamed x9, local copies, waits for them, and re-layouts  7.32 us

profile of v1, /device:TPU:1, one launch (start us, length us, event | category | flops | bytes accessed | tf_op | source)
XLA Modules:
  0.0 81.4 jit_solution(5614780142223883154)
XLA Ops:
  0.6 1.5 %copy.12.left_ref = bf16[2,256,32]{2,1,0:T(8,128)(2,1)} copy(bf16[2,256,32]{1,2,0:T(8,128)(2,1)} %param.15) | data formatting | bytes 65536 | tf_op args[6]
  2.1 1.5 %copy.13.right_ref = bf16[2,256,32]{2,1,0:T(8,128)(2,1)} copy(bf16[2,256,32]{1,2,0:T(8,128)(2,1)} %param.16) | data formatting | bytes 65536 | tf_op args[7]
  3.7 73.4 %shard_map.112 = (f32[2,512,512]{2,1,0:T(8,128)}, f32[2,512]{1,0:T(2,128)}, f32[2,512]{1,0:T(2,128)}) custom-call(s32[2,5]{1,0:T(2,128)} %cols_ref.1, s32[2]{0:T(128)} %count_ref.1, s32[2,6]{1,0:T(2,128)} %far_ref.1, bf16[512,512]{1,0:T(8,128)(2,1)} %src_ref.1, f32[2,512]{1,0:T(2,128)} %self_ref.1, bf16[2,2,5,256,256]{4,3,2,1,0:T(8,128)(2,1)} %tiles_ref.1, ...), custom_call_target="tpu_custom_call" | custom-call | tf_op jit(solution)/shard_map/pallas_call | solution.py:310
  77.1 0.0 copy-start.1
  77.1 0.0 copy-start
  77.2 3.1 %copy.17 = f32[2,512,512]{2,1,0:T(8,128)} copy(f32[2,512,512]{2,1,0:T(8,128)} %get-tuple-element.6) | data formatting | bytes 4194304
  80.2 0.0 copy-done.1
  80.2 0.6 copy.18
  80.8 0.0 copy-done
  80.8 0.6 copy.19
Async XLA Ops:
  77.1 3.1 %copy-start.1 = (f32[2,512]{1,0:T(2,128)S(1)}, f32[2,512]{1,0:T(2,128)}, u32[]{:S(2)}) copy-start(f32[2,512]{1,0:T(2,128)} %get-tuple-element.7) | copy-start | bytes 12292
  77.1 3.7 %copy-start = (f32[2,512]{1,0:T(2,128)S(1)}, f32[2,512]{1,0:T(2,128)}, u32[]{:S(2)}) copy-start(f32[2,512]{1,0:T(2,128)} %get-tuple-element.8) | copy-start | bytes 12292

commit v2 on v1

--- a/solution.py
+++ b/solution.py
@@ -140,18 +140,17 @@
         return remote(part, part, st_send.at[c, t], st_recv.at[c, source], peer)
 
     def to_coeffs(r, values):
-        return lax.dot_general(
-            right_ref[r], values, (((0,), (0,)), ((), ())), preferred_element_type=F32
-        ).astype(BF16)
+        return jnp.dot(right_ref[r], values, preferred_element_type=F32).astype(BF16)
 
     for c in range(chunks):
         cut = pl.ds(c * width, width)
-        u1[c, pl.ds(rows, rows)] = src_ref[:, cut]
-        for copy in halo(u1.at[c], c, h1_send, h1_recv):
-            copy.start()
         for r in range(local):
             z1[c][me * local + r] = to_coeffs(r, src_ref[pl.ds(r * size, size), cut])
         coeff_start(z1, c, z1_send, z1_recv)
+    for c in range(chunks):
+        u1[c, pl.ds(rows, rows)] = src_ref[:, pl.ds(c * width, width)]
+        for copy in halo(u1.at[c], c, h1_send, h1_recv):
+            copy.start()
 
     for r in range(local):
         row = me * local + r
@@ -168,7 +167,7 @@
                 lax.dot_general(
                     coup_ref[o, r, k],
                     left_ref[r],
-                    (((0,), (1,)), ((), ())),
+                    (((0,), (0,)), ((), ())),
                     preferred_element_type=F32,
                 )
                 for k in range(far)
@@ -245,13 +244,14 @@
             norms_ref[pl.ds(o, 1), cut] = norm
             value = ((y_ref[c, o] - h * own) * (inv / norm)).astype(BF16)
             u2[c, o, pl.ds(rows, rows)] = value
-            for copy in halo(u2.at[c, o], 2 * c + o, h2_send, h2_recv):
-                copy.start()
             for r in range(local):
                 z2[c][me * local + r, pl.ds(o * rank, rank)] = to_coeffs(
                     r, value[r * size : (r + 1) * size]
                 )
         coeff_start(z2, c, z2_send, z2_recv)
+        for o in range(2):
+            for copy in halo(u2.at[c, o], 2 * c + o, h2_send, h2_recv):
+                copy.start()
 
     def third(c):
         coeff_forward(z2, c, z2_fsend, z2_recv)
@@ -283,6 +283,12 @@
         @pl.loop(1, devices)
         def _(t):
             stat_copy(c, me, partner, t).wait_send()
+
+
+def hand_over(images_ref, heights_ref, norms_ref, out_images, out_heights, out_norms):
+    out_images[...] = images_ref[...]
+    out_heights[...] = heights_ref[...]
+    out_norms[...] = norms_ref[...]
 
 
 def shards(
@@ -307,7 +313,7 @@
     dma = pltpu.SemaphoreType.DMA
     smem = pl.BlockSpec(memory_space=pltpu.SMEM)
     vmem = pl.BlockSpec(memory_space=pltpu.VMEM)
-    return pl.pallas_call(
+    results = pl.pallas_call(
         functools.partial(kernel, devices),
         out_shape=(
             jax.ShapeDtypeStruct((2, rows, columns), F32),
@@ -350,10 +356,22 @@
         sources,
         self_terms,
         near_tiles,
-        basis_left,
-        basis_right,
+        jnp.swapaxes(basis_left, 1, 2),
+        jnp.swapaxes(basis_right, 1, 2),
         couplings,
     )
+    specs = (
+        pl.BlockSpec((1, rows // 2, columns), lambda o, k: (o, k, 0)),
+        pl.BlockSpec((2, columns), lambda o, k: (0, 0)),
+        pl.BlockSpec((2, columns), lambda o, k: (0, 0)),
+    )
+    return pl.pallas_call(
+        hand_over,
+        grid=(2, 2),
+        out_shape=tuple(jax.ShapeDtypeStruct(r.shape, r.dtype) for r in results),
+        in_specs=specs,
+        out_specs=specs,
+    )(*results)
 
 
 def solution(mesh):

time: 81.7 us -> 76.2 us (0.933)
  local copies, waits for them, and re-layouts: 7.32 us -> 0 us
  Pallas kernels: 73.4 us -> 74.5 us
    unnamed x9 -> x0, local copies, waits for them, and re-layouts: 7.32 us -> none
    pallas_call x0 -> x1, Pallas kernels: none -> 3.8 us  [shards(): pl.pallas_call(hand_over, grid=(2, 2), out_shape=tuple((jax.ShapeDtypeStr...]
    pallas_call x1, Pallas kernels: 73.4 us -> 70.7 us  [shards(): pl.pallas_call(functools.partial(kernel, devices), out_shape=(jax.ShapeDt...]
where the time goes in v2:
time: 76.2 us; the launch traced here: 75.2 us
  Pallas kernels  74.5 us (98%)
    pallas_call x1, Pallas kernels, shards(): pl.pallas_call(functools.partial(kernel, devices), out_shape=(jax.ShapeDt...  70.7 us
    pallas_call x1, Pallas kernels, shards(): pl.pallas_call(hand_over, grid=(2, 2), out_shape=tuple((jax.ShapeDtypeStr...  3.8 us

profile of v2, /device:TPU:1, one launch (start us, length us, event | category | flops | bytes accessed | tf_op | source)
XLA Modules:
  0.0 75.2 jit_solution(12334159768541165358)
XLA Ops:
  0.6 70.7 %shard_map.112 = (f32[2,512,512]{2,1,0:T(8,128)}, f32[2,512]{1,0:T(2,128)}, f32[2,512]{1,0:T(2,128)}) custom-call(s32[2,5]{1,0:T(2,128)} %cols_ref.1, s32[2]{0:T(128)} %count_ref.1, s32[2,6]{1,0:T(2,128)} %far_ref.1, bf16[512,512]{1,0:T(8,128)(2,1)} %src_ref.1, f32[2,512]{1,0:T(2,128)} %self_ref.1, bf16[2,2,5,256,256]{4,3,2,1,0:T(8,128)(2,1)} %tiles_ref.1, ...), custom_call_target="tpu_custom_call" | custom-call | tf_op jit(solution)/shard_map/pallas_call | solution.py:316
  71.3 3.8 %shard_map.113 = (f32[2,512,512]{2,1,0:T(8,128)}, f32[2,512]{1,0:T(2,128)}, f32[2,512]{1,0:T(2,128)}) custom-call(f32[2,512,512]{2,1,0:T(8,128)} %get-tuple-element.6.images_ref, f32[2,512]{1,0:T(2,128)} %get-tuple-element.7.heights_ref, f32[2,512]{1,0:T(2,128)} %get-tuple-element.8.norms_ref), custom_call_target="tpu_custom_call" | custom-call | tf_op jit(solution)/shard_map/pallas_call | solution.py:368
